TPU v7x, 32 devices: a whole 2x2x4 slice. The times are simulated.
32 devices in a mesh: groups: 2 (over y), chan: 4 (over z), tm: 2 (over x), band: 2 (over core).
Axes of the slice: x: 2, y: 2, z: 4, core: 2. Of those that a mesh axis runs over, the one named last changes fastest.
Arguments:
- recording: float32 [1024, 2048], P(('groups', 'chan'), 'tm'), parts along dimension 0, may hold values from -460 to 460
- tau_index: int32 [1024], P(('groups', 'chan')), parts along dimension 0, may hold values from 0 to 7
- pair_offset: int32 [4, 4], replicated, may hold values from -1 to 3, as said below
Outputs:
- correlations: float32 [8, 4, 3, 128, 128], P(('groups', 'chan'), None, None, ('tm', 'band')), parts along dimension 0
There are 2 independent parts, one for each index of `groups`. A program takes and returns all parts, laid end to end along the dimension named above; an argument that names none is the same for every part. Nothing has to cross between parts.
Inputs may be any that keep to these rules, and one draw needn't show every extreme that they name: pair_offset[i, q] is an offset of 1 to 3 blocks for q below the row's partner count, and -1 from there on; every row has 1 to 4 partners.
All inputs are finite; a program needn't handle non-finite values.
Results may differ from a plain program's by a relative error of at most 0.006.
Values may be sent and summed in bfloat16 or wider, within the bound.
A program may use at most 64 MiB of HBM per device.

v0:
```python
import math
import jax
import jax.numpy as jnp
from jax import lax
from jax.sharding import PartitionSpec as P

BLK = 128
HALO_CH = 64
HALO_T = 256
LAGS = 3
QMAX = 4


def from_behind(block, axis, distance):
    devices = range(lax.axis_size(axis))
    route = [(i - distance, i) for i in devices if i - distance in devices]
    return lax.ppermute(block, axis, route)


def padded_2(block, sides, width):
    for axis, dim in sides:
        count = lax.axis_size(axis)
        forward = [(i, i + 1) for i in range(count - 1)]
        backward = [(target, source) for source, target in forward]
        low = lax.ppermute(
            lax.slice_in_dim(block, block.shape[dim] - width, None, axis=dim), axis, forward
        )
        high = lax.ppermute(lax.slice_in_dim(block, 0, width, axis=dim), axis, backward)
        block = jnp.concatenate([low, block, high], axis=dim)
    return block


def slide_total(padded, reach, size, axis):
    zero_shape = list(padded.shape)
    zero_shape[axis] = 1
    running = jnp.concatenate(
        [jnp.zeros(zero_shape, jnp.float32), jnp.cumsum(padded, axis=axis)], axis=axis
    )
    upper = lax.slice_in_dim(running, 2 * reach + 1, 2 * reach + 1 + size, axis=axis)
    lower = lax.slice_in_dim(running, 0, size, axis=axis)
    return upper - lower


def spatial_filter(padded, center, counted):
    total = slide_total(padded, HALO_CH, center.shape[0], 0)
    return center - total / counted[:, None]


def amplitude_norm(padded, center):
    total = slide_total(jnp.abs(padded), HALO_T, center.shape[1], 1)
    return center / (total / (2.0 * HALO_T + 1.0) + 1e-06)


def shards(recording, tau_index, pair_offset):
    channels, samples = recording.shape
    chan_count = lax.axis_size("chan")
    time_count = lax.axis_size("tm")
    band_count = lax.axis_size("band")
    chan_pos = lax.axis_index("chan")
    time_pos = lax.axis_index("tm")
    band_pos = lax.axis_index("band")
    all_channels = channels * chan_count
    all_samples = samples * time_count
    kept_bins = all_samples // 4
    first_bin = kept_bins // 4
    band_bins = kept_bins // band_count
    device_bins = band_bins // time_count
    decay = jnp.exp(-1.0 / (2.0 * 2.0 ** (tau_index.astype(jnp.float32) / 2.0)))[:, None]
    rows_global = chan_pos * channels + jnp.arange(channels)
    counted = (
        jnp.minimum(rows_global, HALO_CH) + jnp.minimum(all_channels - 1 - rows_global, HALO_CH) + 1
    ).astype(jnp.float32)
    previous = from_behind(recording[:, samples - 1 :], "tm", 1)
    deconv = recording - decay * jnp.concatenate([previous, recording[:, : samples - 1]], axis=1)
    deconv_wide = padded_2(deconv, (("chan", 0),), HALO_CH)
    filtered = spatial_filter(deconv_wide, deconv, counted)
    filtered_wide = padded_2(filtered, (("tm", 1),), HALO_T)
    normed = amplitude_norm(filtered_wide, filtered)
    time_global = time_pos * samples + jnp.arange(samples)
    sub_rows = math.gcd(device_bins * lax.axis_size("tm"), 128)
    pieces = device_bins * lax.axis_size("tm") // sub_rows

    def one_piece(piece_idx):
        bins_here = first_bin + band_pos * band_bins + piece_idx * sub_rows + jnp.arange(sub_rows)
        turns = bins_here[:, None] * time_global[None, :] % all_samples
        angle = 2.0 * jnp.pi / all_samples * turns.astype(jnp.float32)
        dims = (((1,), (1,)), ((), ()))
        real_part = lax.dot_general(
            jnp.cos(angle),
            normed,
            dims,
            precision=lax.Precision.HIGHEST,
            preferred_element_type=jnp.float32,
        )
        imag_part = -lax.dot_general(
            jnp.sin(angle),
            normed,
            dims,
            precision=lax.Precision.HIGHEST,
            preferred_element_type=jnp.float32,
        )
        return jnp.stack([real_part, imag_part], axis=1)

    stacked = lax.map(one_piece, jnp.arange(pieces))
    spectra = lax.psum_scatter(
        stacked.reshape(device_bins * lax.axis_size("tm"), 2, channels),
        "tm",
        scatter_dimension=0,
        tiled=True,
    )
    local_power = jnp.sum(spectra * spectra, axis=(0, 1))
    power = lax.psum(local_power, ("tm", "band"))
    factor = lax.rsqrt(power / kept_bins + 1e-06)
    white = (spectra * factor[None, None, :]).astype(jnp.bfloat16)
    bins_mine = first_bin + band_pos * band_bins + time_pos * device_bins + jnp.arange(device_bins)
    lagged = jnp.arange(LAGS) - LAGS // 2
    phase = (
        2.0
        * jnp.pi
        / all_samples
        * (bins_mine[:, None] * lagged[None, :] % all_samples).astype(jnp.float32)
    )
    cosine = jnp.cos(phase)[:, :, None]
    sine = jnp.sin(phase)[:, :, None]
    white_f = white.astype(jnp.float32)
    real_shift = white_f[:, 0, None, :] * cosine - white_f[:, 1, None, :] * sine
    imag_shift = white_f[:, 0, None, :] * sine + white_f[:, 1, None, :] * cosine
    shifted = jnp.stack([real_shift, imag_shift], axis=1).astype(jnp.bfloat16)
    own_blocks = channels // BLK
    all_blocks = all_channels // BLK
    my_offsets = lax.dynamic_slice_in_dim(pair_offset, chan_pos * own_blocks, own_blocks, 0)
    left_blocks = [shifted.reshape(2 * device_bins, LAGS * BLK)]
    cc_scale = 1.0 / math.sqrt(kept_bins)
    initial = tuple(
        (jnp.zeros((LAGS * BLK, BLK), jnp.float32) for slot_all in range(own_blocks * QMAX))
    )
    piece = lax.all_gather(white, "chan", axis=2, tiled=True)
    width = piece.shape[2]
    updated = []
    for slot_idx in range(QMAX):
        offset = my_offsets[0, slot_idx]
        partner = (chan_pos * own_blocks + 0 + jnp.maximum(offset, 0)) % all_blocks
        local_col = partner * BLK
        present = (offset >= 0) & (local_col >= 0) & (local_col < width)
        clipped = jnp.clip(local_col, 0, width - BLK)
        right = lax.dynamic_slice_in_dim(piece, clipped, BLK, 2)
        right = right.reshape(2 * device_bins, BLK)

        def compute(previous_value, left=left_blocks[0], right=right):
            product = lax.dot_general(
                left, right, (((0,), (0,)), ((), ())), preferred_element_type=jnp.float32
            )
            return product * cc_scale

        def keep(previous_value):
            return previous_value

        updated.append(lax.cond(present, compute, keep, initial[slot_idx]))
    gathered = tuple(updated)
    stacked_cc = jnp.stack(gathered).reshape(own_blocks, QMAX, LAGS, BLK, BLK)
    return lax.psum_scatter(stacked_cc, ("tm", "band"), scatter_dimension=3, tiled=True)


def solution(mesh):
    return jax.shard_map(
        shards,
        mesh=mesh,
        in_specs=(P(("groups", "chan"), "tm"), P(("groups", "chan")), P()),
        out_specs=P(("groups", "chan"), None, None, ("tm", "band"), None),
        check_vma=False,
    )
```

profile of v0, /device:TPU:0, one launch (start us, length us, event | category | flops | bytes accessed | tf_op | source)
XLA Modules:
  0.0 122.5 jit_solution(3115787574492478725)
XLA Ops:
  6.5 0.9 slice.63
  7.5 4.8 %collective-permute-start = (f32[128,1]{1,0:T(8,128)S(1)}, f32[128,1]{1,0:T(8,128)S(1)}, u32[]{:S(2)}, u32[]{:S(2)}) collective-permute-start(f32[128,1]{1,0:T(8,128)S(1)} %slice.63), channel_id=1, source_target_pairs={{0,2},{1,3},{4,6},{5,7},{8,10},{9,11},{12,14},{13,15},{16,18},{17,... | collective-permute-start | bytes 1544 | tf_op jit(solution)/shard_map/ppermute | solution.py:17
  13.0 1.2 collective-permute-done
  14.2 1.4 %fusion.34 = f32[128,1024]{1,0:T(8,128)S(1)} fusion(f32[128,1024]{1,0:T(8,128)} %param.13, f32[128,1023]{1,0:T(8,128)} %bitcast.94, f32[128,1]{1,0:T(8,128)S(1)} %collective-permute-done, f32[128]{0:T(128)S(1)} %divide_exponential_fusion), kind=kLoop, calls=%fused_computation.55 | loop fusion | flops 393216 | bytes 1573376 | tf_op jit(solution)/shard_map/sub | solution.py:74
  15.7 3.5 %collective-permute-start.1 = (f32[64,1024]{1,0:T(8,128)S(1)}, f32[64,1024]{1,0:T(8,128)S(1)}, u32[]{:S(2)}, u32[]{:S(2)}) collective-permute-start(f32[64,1024]{1,0:T(8,128)S(1)} %get-tuple-element.262), channel_id=1, source_target_pairs={{0,4},{4,8},{8,12},{1,5},{5,9},{9,13},{2,6},{6,10},{10,14},{3,7},{... | collective-permute-start | bytes 786440 | tf_op jit(solution)/shard_map/ppermute | solution.py:25
  19.2 1.3 %collective-permute-start.2 = (f32[64,1024]{1,0:T(8,128)S(1)}, f32[64,1024]{1,0:T(8,128)S(1)}, u32[]{:S(2)}, u32[]{:S(2)}) collective-permute-start(f32[64,1024]{1,0:T(8,128)S(1)} %get-tuple-element.263), channel_id=1, source_target_pairs={{4,0},{8,4},{12,8},{5,1},{9,5},{13,9},{6,2},{10,6},{14,10},{7,3},{... | collective-permute-start | bytes 786440 | tf_op jit(solution)/shard_map/ppermute | solution.py:28
  20.5 3.4 %collective-permute-done.1 = f32[64,1024]{1,0:T(8,128)S(1)} collective-permute-done((f32[64,1024]{1,0:T(8,128)S(1)}, f32[64,1024]{1,0:T(8,128)S(1)}, u32[]{:S(2)}, u32[]{:S(2)}) %collective-permute-start.1) | collective-permute-done | bytes 262176 | tf_op jit(solution)/shard_map/ppermute | solution.py:25
  23.9 4.1 %collective-permute-done.2 = f32[64,1024]{1,0:T(8,128)S(1)} collective-permute-done((f32[64,1024]{1,0:T(8,128)S(1)}, f32[64,1024]{1,0:T(8,128)S(1)}, u32[]{:S(2)}, u32[]{:S(2)}) %collective-permute-start.2) | collective-permute-done | bytes 262176 | tf_op jit(solution)/shard_map/ppermute | solution.py:28
  29.6 4.0 %collective-permute-start.3 = (f32[128,256]{1,0:T(8,128)S(1)}, f32[128,256]{1,0:T(8,128)S(1)}, u32[]{:S(2)}, u32[]{:S(2)}) collective-permute-start(f32[128,256]{1,0:T(8,128)S(1)} %get-tuple-element.260), channel_id=1, source_target_pairs={{0,2},{1,3},{4,6},{5,7},{8,10},{9,11},{12,14},{13,15},{16,18},{17,... | collective-permute-start | bytes 393224 | tf_op jit(solution)/shard_map/ppermute | solution.py:25
  33.6 1.3 %collective-permute-start.4 = (f32[128,256]{1,0:T(8,128)S(1)}, f32[128,256]{1,0:T(8,128)S(1)}, u32[]{:S(2)}, u32[]{:S(2)}) collective-permute-start(f32[128,256]{1,0:T(8,128)S(1)} %get-tuple-element.261), channel_id=1, source_target_pairs={{2,0},{3,1},{6,4},{7,5},{10,8},{11,9},{14,12},{15,13},{18,16},{19,... | collective-permute-start | bytes 393224 | tf_op jit(solution)/shard_map/ppermute | solution.py:28
  34.9 1.2 collective-permute-done.3
  36.0 4.4 %collective-permute-done.4 = f32[128,256]{1,0:T(8,128)S(1)} collective-permute-done((f32[128,256]{1,0:T(8,128)S(1)}, f32[128,256]{1,0:T(8,128)S(1)}, u32[]{:S(2)}, u32[]{:S(2)}) %collective-permute-start.4) | collective-permute-done | bytes 131104 | tf_op jit(solution)/shard_map/ppermute | solution.py:28
  42.1 13.2 %while.13 = (s32[]{:T(128)}, f32[2,128,2,128]{3,1,0,2:T(8,128)S(1)}, s32[2]{0:T(128)S(1)}, s32[]{:T(128)}, f32[128,1024]{1,0:T(8,128)S(1)}, /*index=5*/s32[]{:T(128)}, s32[]{:T(128)}, s32[1]{0:T(128)}) while((s32[]{:T(128)}, f32[2,128,2,128]{3,1,0,2:T(8,128)S(1)}, s32[2]{0:T(128)S(1)}, s32[]{:T(128)}, f32[128,1024]{1,0:T(8,128)S(1)}, ...), condition=%wide.region_5.6_spmd.clone, body=%wide.region_4.5_spmd.clone.sunk | while | flops 406373504 | bytes 1455749 | solution.py:104
  43.5 2.6 %convolution_bitcast_fusion.2 = f32[128,1,128]{2,0,1:T(8,128)S(1)} fusion(f32[128,1024]{1,0:T(8,128)S(1)} %get-tuple-element.331, s32[1024]{0:T(1024)S(1)} %iota_add_fusion.6, s32[128]{0:T(128)S(1)} %iota_add_fusion.7), kind=kOutput, calls=%fused_computation.15.clone.1 | convolution fusion | flops 203161600 | bytes 594432 | tf_op jit(solution)/shard_map/while/body/eval_jaxpr/dot_general | solution.py:88
  46.1 2.6 %fusion.64 = f32[128,1,128]{2,0,1:T(8,128)S(1)} fusion(f32[128,1024]{1,0:T(8,128)S(1)} %get-tuple-element.331, s32[1024]{0:T(1024)S(1)} %iota_add_fusion.6, s32[128]{0:T(128)S(1)} %iota_add_fusion.7), kind=kOutput, calls=%fused_computation.14.clone.1 | convolution fusion | flops 203177984 | bytes 594432 | tf_op jit(solution)/shard_map/while/body/eval_jaxpr/dot_general | solution.py:95
  50.1 2.6 %convolution_bitcast_fusion.2 = f32[128,1,128]{2,0,1:T(8,128)S(1)} fusion(f32[128,1024]{1,0:T(8,128)S(1)} %get-tuple-element.331, s32[1024]{0:T(1024)S(1)} %iota_add_fusion.6, s32[128]{0:T(128)S(1)} %iota_add_fusion.7), kind=kOutput, calls=%fused_computation.15.clone.1 | convolution fusion | flops 203161600 | bytes 594432 | tf_op jit(solution)/shard_map/while/body/eval_jaxpr/dot_general | solution.py:88
  52.7 2.6 %fusion.64 = f32[128,1,128]{2,0,1:T(8,128)S(1)} fusion(f32[128,1024]{1,0:T(8,128)S(1)} %get-tuple-element.331, s32[1024]{0:T(1024)S(1)} %iota_add_fusion.6, s32[128]{0:T(128)S(1)} %iota_add_fusion.7), kind=kOutput, calls=%fused_computation.14.clone.1 | convolution fusion | flops 203177984 | bytes 594432 | tf_op jit(solution)/shard_map/while/body/eval_jaxpr/dot_general | solution.py:95
  62.3 4.9 %reduce-scatter.3.cloned.1.call-done = f32[128,2,128]{2,0,1:T(8,128)} async-done(((f32[256,2,128]{2,0,1:T(8,128)}), f32[128,2,128]{2,0,1:T(8,128)}) %reduce-scatter.3.cloned.1.call-update) | async-done | bytes 131088 | tf_op jit(solution)/shard_map/reduce_scatter | solution.py:105
  67.1 1.0 multiply_reduce_fusion
  68.1 5.8 %psum.7 = f32[128]{0:T(128)S(1)} all-reduce(f32[128]{0:T(128)S(1)} %multiply_reduce_fusion), channel_id=1, replica_groups=mesh['groups'=2,'chan'=4,'tm'=2,'band'=2] {'tm','band'}, use_global_device_ids=true, to_apply=%region_8.9 | all-reduce | flops 128 | bytes 1024 | tf_op jit(solution)/shard_map/psum | solution.py:112
  73.9 0.9 fusion.40
  75.4 13.0 %all_gather.3 = bf16[128,2,512]{2,0,1:T(8,128)(2,1)S(1)} all-gather(bf16[128,2,128]{2,0,1:T(8,128)(2,1)S(1)} %get-tuple-element.259), channel_id=1, replica_groups=mesh['groups'=2,'chan'=4,'tm'=2,'band'=2] {'chan'}, dimensions={2}, use_global_device_ids=true | all-gather | bytes 327680 | tf_op jit(solution)/shard_map/all_gather | solution.py:137
  91.6 1.0 pad_maximum_fusion.1
  92.6 23.1 %reduce-scatter.5.cloned.1.call-done = f32[1,4,3,32,128]{4,3,2,1,0:T(8,128)} async-done(((f32[1,4,3,128,128]{4,3,2,1,0:T(8,128)}), f32[1,4,3,32,128]{4,3,2,1,0:T(8,128)}) %reduce-scatter.5.cloned.1.call-update) | async-done | bytes 196624 | tf_op jit(solution)/shard_map/reduce_scatter | solution.py:161
  (72 shorter events, 13.8 us)
Async XLA Ops:
  6.5 28.3 %copy-start = (s32[4,4]{1,0:T(4,128)S(1)}, s32[4,4]{1,0:T(4,128)}, u32[]{:S(2)}) copy-start(s32[4,4]{1,0:T(4,128)} %param.15) | copy-start | bytes 196
  6.5 60.6 %reduce-scatter.3.cloned.1.call-start = ((), (), s32[]{:S(2)}) async-start(), calls=%async_computation.2 | async-start | bytes 393216 | tf_op jit(solution)/shard_map/reduce_scatter | solution.py:105
  7.5 6.7 %collective-permute-start = (f32[128,1]{1,0:T(8,128)S(1)}, f32[128,1]{1,0:T(8,128)S(1)}, u32[]{:S(2)}, u32[]{:S(2)}) collective-permute-start(f32[128,1]{1,0:T(8,128)S(1)} %slice.63), channel_id=1, source_target_pairs={{0,2},{1,3},{4,6},{5,7},{8,10},{9,11},{12,14},{13,15},{16,18},{17,... | collective-permute-start | bytes 1544 | tf_op jit(solution)/shard_map/ppermute | solution.py:17
  15.7 8.2 %collective-permute-start.1 = (f32[64,1024]{1,0:T(8,128)S(1)}, f32[64,1024]{1,0:T(8,128)S(1)}, u32[]{:S(2)}, u32[]{:S(2)}) collective-permute-start(f32[64,1024]{1,0:T(8,128)S(1)} %get-tuple-element.262), channel_id=1, source_target_pairs={{0,4},{4,8},{8,12},{1,5},{5,9},{9,13},{2,6},{6,10},{10,14},{3,7},{... | collective-permute-start | bytes 786440 | tf_op jit(solution)/shard_map/ppermute | solution.py:25
  19.2 8.8 %collective-permute-start.2 = (f32[64,1024]{1,0:T(8,128)S(1)}, f32[64,1024]{1,0:T(8,128)S(1)}, u32[]{:S(2)}, u32[]{:S(2)}) collective-permute-start(f32[64,1024]{1,0:T(8,128)S(1)} %get-tuple-element.263), channel_id=1, source_target_pairs={{4,0},{8,4},{12,8},{5,1},{9,5},{13,9},{6,2},{10,6},{14,10},{7,3},{... | collective-permute-start | bytes 786440 | tf_op jit(solution)/shard_map/ppermute | solution.py:28
  29.6 6.5 %collective-permute-start.3 = (f32[128,256]{1,0:T(8,128)S(1)}, f32[128,256]{1,0:T(8,128)S(1)}, u32[]{:S(2)}, u32[]{:S(2)}) collective-permute-start(f32[128,256]{1,0:T(8,128)S(1)} %get-tuple-element.260), channel_id=1, source_target_pairs={{0,2},{1,3},{4,6},{5,7},{8,10},{9,11},{12,14},{13,15},{16,18},{17,... | collective-permute-start | bytes 393224 | tf_op jit(solution)/shard_map/ppermute | solution.py:25
  33.6 6.9 %collective-permute-start.4 = (f32[128,256]{1,0:T(8,128)S(1)}, f32[128,256]{1,0:T(8,128)S(1)}, u32[]{:S(2)}, u32[]{:S(2)}) collective-permute-start(f32[128,256]{1,0:T(8,128)S(1)} %get-tuple-element.261), channel_id=1, source_target_pairs={{2,0},{3,1},{6,4},{7,5},{10,8},{11,9},{14,12},{15,13},{18,16},{19,... | collective-permute-start | bytes 393224 | tf_op jit(solution)/shard_map/ppermute | solution.py:28
  55.3 0.7 copy-start.1
  56.0 59.6 %reduce-scatter.5.cloned.1.call-start = ((), (), s32[]{:S(2)}) async-start(), calls=%async_computation.3 | async-start | bytes 983040 | tf_op jit(solution)/shard_map/reduce_scatter | solution.py:161
Sparse Core Ops, SparseCore 0:
  56.1 10.9 reduce-scatter.2
  92.7 22.9 reduce-scatter.4
where the time goes:
time: 123 us
  waiting for transfers between devices  42.2 us (34%)
  between operations  18.9 us (15%)
  blocking collectives  18.8 us (15%)
  starting transfers between devices  14.9 us (12%)
  matrix products  11.1 us (9%)
  other arithmetic  7.65 us (6%)
  local copies, waits for them, and re-layouts  7.28 us (6%)
  loops' own time  1.66 us (1%)
    reduce_scatter x1, waiting for transfers between devices, shards(): lax.psum_scatter(stacked_cc, ('tm', 'band'), scatter_dimension=3, tiled=T...  23.1 us
    all_gather x1, blocking collectives, shards(): piece = lax.all_gather(white, 'chan', axis=2, tiled=True)  13 us
    ppermute x2, waiting for transfers between devices, padded_2(): lax.ppermute(lax.slice_in_dim(block, 0, width, axis=dim), axis, backward)  8.49 us
    ppermute x2, starting transfers between devices, padded_2(): lax.ppermute(lax.slice_in_dim(block, block.shape[dim] - width, None, axis...  7.47 us
    psum x1, blocking collectives, shards(): power = lax.psum(local_power, ('tm', 'band'))  5.75 us
    dot_general x2, matrix products, one_piece(): lax.dot_general(jnp.sin(angle), normed, dims, precision=lax.Precision.HIG...  5.16 us
    dot_general x2, matrix products, one_piece(): lax.dot_general(jnp.cos(angle), normed, dims, precision=lax.Precision.HIG...  5.13 us
    reduce_scatter x1, waiting for transfers between devices, shards(): lax.psum_scatter(stacked.reshape(device_bins * lax.axis_size('tm'), 2, ch...  4.85 us
  transfers between devices with their start and end apart: 7, of which 7 were waited for; matrix products, arithmetic and copies ran while one was open for 1% of the time, Pallas kernels for 0%

commit v1 on v0

--- a/solution.py
+++ b/solution.py
@@ -134,7 +134,15 @@
     initial = tuple(
         (jnp.zeros((LAGS * BLK, BLK), jnp.float32) for slot_all in range(own_blocks * QMAX))
     )
-    piece = lax.all_gather(white, "chan", axis=2, tiled=True)
+    ways, here, step = (lax.axis_size("chan"), lax.axis_index("chan"), white.shape[2])
+    line, have = (white, 1)
+    while have < ways:
+        line = jnp.concatenate(
+            [line, lax.ppermute(line, "chan", [(d, (d - have) % ways) for d in range(ways)])],
+            axis=2,
+        )
+        have = 2 * have
+    piece = jnp.roll(line, here * step, axis=2)
     width = piece.shape[2]
     updated = []
     for slot_idx in range(QMAX):

time: 123 us -> 125 us (1.016)
  blocking collectives: 18.8 us -> 5.75 us
  waiting for transfers between devices: 42.2 us -> 50.8 us
  starting transfers between devices: 14.9 us -> 20 us
    all_gather x1 -> x0, blocking collectives: 13 us -> none  [shards(): piece = lax.all_gather(white, 'chan', axis=2, tiled=True)]
    ppermute x0 -> x2, waiting for transfers between devices: none -> 7.68 us  [shards(): lax.ppermute(line, 'chan', [(d, (d - have) % ways) for d in range(ways)])]
    ppermute x0 -> x2, starting transfers between devices: none -> 5.07 us  [shards(): lax.ppermute(line, 'chan', [(d, (d - have) % ways) for d in range(ways)])]
  transfers between devices with their start and end apart: 7 -> 9, of which waited for: 7 -> 9; matrix products, arithmetic and copies ran while one was open for 1% -> 2% of each run, Pallas kernels for 0% -> 0%
where the time goes in v1:
time: 125 us; the launch traced here: 124 us
  waiting for transfers between devices  50.8 us (41%)
  starting transfers between devices  20 us (16%)
  between operations  18.8 us (15%)
  matrix products  11.1 us (9%)
  local copies, waits for them, and re-layouts  8.4 us (7%)
  other arithmetic  7.66 us (6%)
  blocking collectives  5.75 us (5%)
  loops' own time  1.89 us (2%)
    reduce_scatter x1, waiting for transfers between devices, shards(): lax.psum_scatter(stacked_cc, ('tm', 'band'), scatter_dimension=3, tiled=T...  23.9 us
    ppermute x2, waiting for transfers between devices, padded_2(): lax.ppermute(lax.slice_in_dim(block, 0, width, axis=dim), axis, backward)  8.49 us
    ppermute x2, waiting for transfers between devices, shards(): lax.ppermute(line, 'chan', [(d, (d - have) % ways) for d in range(ways)])  7.68 us
    ppermute x2, starting transfers between devices, padded_2(): lax.ppermute(lax.slice_in_dim(block, block.shape[dim] - width, None, axis...  7.47 us
    psum x1, blocking collectives, shards(): power = lax.psum(local_power, ('tm', 'band'))  5.75 us
    dot_general x2, matrix products, one_piece(): lax.dot_general(jnp.sin(angle), normed, dims, precision=lax.Precision.HIG...  5.16 us
    dot_general x2, matrix products, one_piece(): lax.dot_general(jnp.cos(angle), normed, dims, precision=lax.Precision.HIG...  5.14 us
    ppermute x2, starting transfers between devices, shards(): lax.ppermute(line, 'chan', [(d, (d - have) % ways) for d in range(ways)])  5.07 us
  transfers between devices with their start and end apart: 9, of which 9 were waited for; matrix products, arithmetic and copies ran while one was open for 2% of the time, Pallas kernels for 0%

profile of v1, /device:TPU:0, one launch (start us, length us, event | category | flops | bytes accessed | tf_op | source)
XLA Modules:
  0.0 124.4 jit_solution(16460726585812545766)
XLA Ops:
  7.5 4.8 %collective-permute-start = (f32[128,1]{1,0:T(8,128)S(1)}, f32[128,1]{1,0:T(8,128)S(1)}, u32[]{:S(2)}, u32[]{:S(2)}) collective-permute-start(f32[128,1]{1,0:T(8,128)S(1)} %slice.63), channel_id=1, source_target_pairs={{0,2},{1,3},{4,6},{5,7},{8,10},{9,11},{12,14},{13,15},{16,18},{17,... | collective-permute-start | bytes 1544 | tf_op jit(solution)/shard_map/ppermute | solution.py:17
  13.0 1.2 collective-permute-done
  14.2 1.4 %fusion.34 = f32[128,1024]{1,0:T(8,128)S(1)} fusion(f32[128,1024]{1,0:T(8,128)} %param.13, f32[128,1023]{1,0:T(8,128)} %bitcast.94, f32[128,1]{1,0:T(8,128)S(1)} %collective-permute-done, f32[128]{0:T(128)S(1)} %divide_exponential_fusion), kind=kLoop, calls=%fused_computation.55 | loop fusion | flops 393216 | bytes 1573376 | tf_op jit(solution)/shard_map/sub | solution.py:74
  15.7 3.5 %collective-permute-start.1 = (f32[64,1024]{1,0:T(8,128)S(1)}, f32[64,1024]{1,0:T(8,128)S(1)}, u32[]{:S(2)}, u32[]{:S(2)}) collective-permute-start(f32[64,1024]{1,0:T(8,128)S(1)} %get-tuple-element.322), channel_id=1, source_target_pairs={{0,4},{4,8},{8,12},{1,5},{5,9},{9,13},{2,6},{6,10},{10,14},{3,7},{... | collective-permute-start | bytes 786440 | tf_op jit(solution)/shard_map/ppermute | solution.py:25
  19.2 1.3 %collective-permute-start.2 = (f32[64,1024]{1,0:T(8,128)S(1)}, f32[64,1024]{1,0:T(8,128)S(1)}, u32[]{:S(2)}, u32[]{:S(2)}) collective-permute-start(f32[64,1024]{1,0:T(8,128)S(1)} %get-tuple-element.323), channel_id=1, source_target_pairs={{4,0},{8,4},{12,8},{5,1},{9,5},{13,9},{6,2},{10,6},{14,10},{7,3},{... | collective-permute-start | bytes 786440 | tf_op jit(solution)/shard_map/ppermute | solution.py:28
  20.5 3.4 %collective-permute-done.1 = f32[64,1024]{1,0:T(8,128)S(1)} collective-permute-done((f32[64,1024]{1,0:T(8,128)S(1)}, f32[64,1024]{1,0:T(8,128)S(1)}, u32[]{:S(2)}, u32[]{:S(2)}) %collective-permute-start.1) | collective-permute-done | bytes 262176 | tf_op jit(solution)/shard_map/ppermute | solution.py:25
  23.9 4.1 %collective-permute-done.2 = f32[64,1024]{1,0:T(8,128)S(1)} collective-permute-done((f32[64,1024]{1,0:T(8,128)S(1)}, f32[64,1024]{1,0:T(8,128)S(1)}, u32[]{:S(2)}, u32[]{:S(2)}) %collective-permute-start.2) | collective-permute-done | bytes 262176 | tf_op jit(solution)/shard_map/ppermute | solution.py:28
  29.6 4.0 %collective-permute-start.3 = (f32[128,256]{1,0:T(8,128)S(1)}, f32[128,256]{1,0:T(8,128)S(1)}, u32[]{:S(2)}, u32[]{:S(2)}) collective-permute-start(f32[128,256]{1,0:T(8,128)S(1)} %get-tuple-element.320), channel_id=1, source_target_pairs={{0,2},{1,3},{4,6},{5,7},{8,10},{9,11},{12,14},{13,15},{16,18},{17,... | collective-permute-start | bytes 393224 | tf_op jit(solution)/shard_map/ppermute | solution.py:25
  33.6 1.3 %collective-permute-start.4 = (f32[128,256]{1,0:T(8,128)S(1)}, f32[128,256]{1,0:T(8,128)S(1)}, u32[]{:S(2)}, u32[]{:S(2)}) collective-permute-start(f32[128,256]{1,0:T(8,128)S(1)} %get-tuple-element.321), channel_id=1, source_target_pairs={{2,0},{3,1},{6,4},{7,5},{10,8},{11,9},{14,12},{15,13},{18,16},{19,... | collective-permute-start | bytes 393224 | tf_op jit(solution)/shard_map/ppermute | solution.py:28
  34.9 1.2 collective-permute-done.3
  36.0 4.4 %collective-permute-done.4 = f32[128,256]{1,0:T(8,128)S(1)} collective-permute-done((f32[128,256]{1,0:T(8,128)S(1)}, f32[128,256]{1,0:T(8,128)S(1)}, u32[]{:S(2)}, u32[]{:S(2)}) %collective-permute-start.4) | collective-permute-done | bytes 131104 | tf_op jit(solution)/shard_map/ppermute | solution.py:28
  42.1 13.1 %while.13 = (s32[]{:T(128)}, f32[2,128,2,128]{3,1,0,2:T(8,128)S(1)}, s32[2]{0:T(128)S(1)}, s32[]{:T(128)}, f32[128,1024]{1,0:T(8,128)S(1)}, /*index=5*/s32[]{:T(128)}, s32[]{:T(128)}, s32[1]{0:T(128)}) while((s32[]{:T(128)}, f32[2,128,2,128]{3,1,0,2:T(8,128)S(1)}, s32[2]{0:T(128)S(1)}, s32[]{:T(128)}, f32[128,1024]{1,0:T(8,128)S(1)}, ...), condition=%wide.region_5.6_spmd.clone, body=%wide.region_4.5_spmd.clone.sunk | while | flops 406373504 | bytes 1455749 | solution.py:104
  43.5 2.6 %convolution_bitcast_fusion.2 = f32[128,1,128]{2,0,1:T(8,128)S(1)} fusion(f32[128,1024]{1,0:T(8,128)S(1)} %get-tuple-element.391, s32[1024]{0:T(1024)S(1)} %iota_add_fusion.6, s32[128]{0:T(128)S(1)} %iota_add_fusion.7), kind=kOutput, calls=%fused_computation.15.clone.1 | convolution fusion | flops 203161600 | bytes 594432 | tf_op jit(solution)/shard_map/while/body/eval_jaxpr/dot_general | solution.py:88
  46.1 2.6 %fusion.64 = f32[128,1,128]{2,0,1:T(8,128)S(1)} fusion(f32[128,1024]{1,0:T(8,128)S(1)} %get-tuple-element.391, s32[1024]{0:T(1024)S(1)} %iota_add_fusion.6, s32[128]{0:T(128)S(1)} %iota_add_fusion.7), kind=kOutput, calls=%fused_computation.14.clone.1 | convolution fusion | flops 203177984 | bytes 594432 | tf_op jit(solution)/shard_map/while/body/eval_jaxpr/dot_general | solution.py:95
  50.1 2.6 %convolution_bitcast_fusion.2 = f32[128,1,128]{2,0,1:T(8,128)S(1)} fusion(f32[128,1024]{1,0:T(8,128)S(1)} %get-tuple-element.391, s32[1024]{0:T(1024)S(1)} %iota_add_fusion.6, s32[128]{0:T(128)S(1)} %iota_add_fusion.7), kind=kOutput, calls=%fused_computation.15.clone.1 | convolution fusion | flops 203161600 | bytes 594432 | tf_op jit(solution)/shard_map/while/body/eval_jaxpr/dot_general | solution.py:88
  52.6 2.6 %fusion.64 = f32[128,1,128]{2,0,1:T(8,128)S(1)} fusion(f32[128,1024]{1,0:T(8,128)S(1)} %get-tuple-element.391, s32[1024]{0:T(1024)S(1)} %iota_add_fusion.6, s32[128]{0:T(128)S(1)} %iota_add_fusion.7), kind=kOutput, calls=%fused_computation.14.clone.1 | convolution fusion | flops 203177984 | bytes 594432 | tf_op jit(solution)/shard_map/while/body/eval_jaxpr/dot_general | solution.py:95
  62.1 5.0 %reduce-scatter.3.cloned.1.call-done = f32[128,2,128]{2,0,1:T(8,128)} async-done(((f32[256,2,128]{2,0,1:T(8,128)}), f32[128,2,128]{2,0,1:T(8,128)}) %reduce-scatter.3.cloned.1.call-update) | async-done | bytes 131088 | tf_op jit(solution)/shard_map/reduce_scatter | solution.py:105
  68.1 5.8 %psum.7 = f32[128]{0:T(128)S(1)} all-reduce(f32[128]{0:T(128)S(1)} %multiply_reduce_fusion), channel_id=1, replica_groups=mesh['groups'=2,'chan'=4,'tm'=2,'band'=2] {'tm','band'}, use_global_device_ids=true, to_apply=%region_8.9 | all-reduce | flops 128 | bytes 1024 | tf_op jit(solution)/shard_map/psum | solution.py:112
  74.8 3.6 %collective-permute-start.5 = (bf16[128,2,128]{2,0,1:T(8,128)(2,1)S(1)}, bf16[128,2,128]{2,0,1:T(8,128)(2,1)S(1)}, u32[]{:S(2)}, u32[]{:S(2)}) collective-permute-start(bf16[128,2,128]{2,0,1:T(8,128)(2,1)S(1)} %get-tuple-element.319), channel_id=1, source_target_pairs={{0,12},{4,0},{8,4},{12,8},{1,13},{5,1},{9,5},{13,9},{2,14},{6,2},{... | collective-permute-start | bytes 196616 | tf_op jit(solution)/shard_map/ppermute | solution.py:141
  78.9 1.4 %collective-permute-done.5 = bf16[128,2,128]{2,0,1:T(8,128)(2,1)S(1)} collective-permute-done((bf16[128,2,128]{2,0,1:T(8,128)(2,1)S(1)}, bf16[128,2,128]{2,0,1:T(8,128)(2,1)S(1)}, u32[]{:S(2)}, u32[]{:S(2)}) %collective-permute-start.5) | collective-permute-done | bytes 65568 | tf_op jit(solution)/shard_map/ppermute | solution.py:141
  80.3 1.5 %collective-permute-start.6 = (bf16[128,2,256]{2,0,1:T(8,128)(2,1)S(1)}, bf16[128,2,256]{2,0,1:T(8,128)(2,1)S(1)}, u32[]{:S(2)}, u32[]{:S(2)}) collective-permute-start(bf16[128,2,256]{2,0,1:T(8,128)(2,1)S(1)} %pad_maximum_fusion.3), channel_id=1, source_target_pairs={{0,8},{4,12},{8,0},{12,4},{1,9},{5,13},{9,1},{13,5},{2,10},{6,14},... | collective-permute-start | bytes 393224 | tf_op jit(solution)/shard_map/ppermute | solution.py:141
  81.8 6.3 %collective-permute-done.6 = bf16[128,2,256]{2,0,1:T(8,128)(2,1)S(1)} collective-permute-done((bf16[128,2,256]{2,0,1:T(8,128)(2,1)S(1)}, bf16[128,2,256]{2,0,1:T(8,128)(2,1)S(1)}, u32[]{:S(2)}, u32[]{:S(2)}) %collective-permute-start.6) | collective-permute-done | bytes 131104 | tf_op jit(solution)/shard_map/ppermute | solution.py:141
  89.3 1.3 %conditional.5 = (f32[1,1,3,128,128]{4,3,2,1,0:T(8,128)S(1)}) conditional(s32[]{:T(128)} %convert_element_type.56, () %tuple.60, (s32[]{:T(128)}, s32[]{:T(128)}, bf16[128,2,1024]{2,0,1:T(8,128)(2,1)S(1)}, bf16[256,384]{1,0:T(8,128)(2,1)S(1)}) %tuple.110), branch_computations={%region_11.12_spmd, %region_12.13_spmd} | conditional | flops 25214980 | bytes 2031680 | solution.py:166
  93.7 23.9 %reduce-scatter.5.cloned.1.call-done = f32[1,4,3,32,128]{4,3,2,1,0:T(8,128)} async-done(((f32[1,4,3,128,128]{4,3,2,1,0:T(8,128)}), f32[1,4,3,32,128]{4,3,2,1,0:T(8,128)}) %reduce-scatter.5.cloned.1.call-update) | async-done | bytes 196624 | tf_op jit(solution)/shard_map/reduce_scatter | solution.py:169
  (82 shorter events, 18.8 us)
Async XLA Ops:
  6.5 28.3 %copy-start = (s32[4,4]{1,0:T(4,128)S(1)}, s32[4,4]{1,0:T(4,128)}, u32[]{:S(2)}) copy-start(s32[4,4]{1,0:T(4,128)} %param.15) | copy-start | bytes 196
  6.5 60.6 %reduce-scatter.3.cloned.1.call-start = ((), (), s32[]{:S(2)}) async-start(), calls=%async_computation.2 | async-start | bytes 393216 | tf_op jit(solution)/shard_map/reduce_scatter | solution.py:105
  7.5 6.7 %collective-permute-start = (f32[128,1]{1,0:T(8,128)S(1)}, f32[128,1]{1,0:T(8,128)S(1)}, u32[]{:S(2)}, u32[]{:S(2)}) collective-permute-start(f32[128,1]{1,0:T(8,128)S(1)} %slice.63), channel_id=1, source_target_pairs={{0,2},{1,3},{4,6},{5,7},{8,10},{9,11},{12,14},{13,15},{16,18},{17,... | collective-permute-start | bytes 1544 | tf_op jit(solution)/shard_map/ppermute | solution.py:17
  15.7 8.2 %collective-permute-start.1 = (f32[64,1024]{1,0:T(8,128)S(1)}, f32[64,1024]{1,0:T(8,128)S(1)}, u32[]{:S(2)}, u32[]{:S(2)}) collective-permute-start(f32[64,1024]{1,0:T(8,128)S(1)} %get-tuple-element.322), channel_id=1, source_target_pairs={{0,4},{4,8},{8,12},{1,5},{5,9},{9,13},{2,6},{6,10},{10,14},{3,7},{... | collective-permute-start | bytes 786440 | tf_op jit(solution)/shard_map/ppermute | solution.py:25
  19.2 8.8 %collective-permute-start.2 = (f32[64,1024]{1,0:T(8,128)S(1)}, f32[64,1024]{1,0:T(8,128)S(1)}, u32[]{:S(2)}, u32[]{:S(2)}) collective-permute-start(f32[64,1024]{1,0:T(8,128)S(1)} %get-tuple-element.323), channel_id=1, source_target_pairs={{4,0},{8,4},{12,8},{5,1},{9,5},{13,9},{6,2},{10,6},{14,10},{7,3},{... | collective-permute-start | bytes 786440 | tf_op jit(solution)/shard_map/ppermute | solution.py:28
  29.6 6.5 %collective-permute-start.3 = (f32[128,256]{1,0:T(8,128)S(1)}, f32[128,256]{1,0:T(8,128)S(1)}, u32[]{:S(2)}, u32[]{:S(2)}) collective-permute-start(f32[128,256]{1,0:T(8,128)S(1)} %get-tuple-element.320), channel_id=1, source_target_pairs={{0,2},{1,3},{4,6},{5,7},{8,10},{9,11},{12,14},{13,15},{16,18},{17,... | collective-permute-start | bytes 393224 | tf_op jit(solution)/shard_map/ppermute | solution.py:25
  33.6 6.9 %collective-permute-start.4 = (f32[128,256]{1,0:T(8,128)S(1)}, f32[128,256]{1,0:T(8,128)S(1)}, u32[]{:S(2)}, u32[]{:S(2)}) collective-permute-start(f32[128,256]{1,0:T(8,128)S(1)} %get-tuple-element.321), channel_id=1, source_target_pairs={{2,0},{3,1},{6,4},{7,5},{10,8},{11,9},{14,12},{15,13},{18,16},{19,... | collective-permute-start | bytes 393224 | tf_op jit(solution)/shard_map/ppermute | solution.py:28
  55.3 0.7 copy-start.1
  56.0 61.6 %reduce-scatter.5.cloned.1.call-start = ((), (), s32[]{:S(2)}) async-start(), calls=%async_computation.3 | async-start | bytes 983040 | tf_op jit(solution)/shard_map/reduce_scatter | solution.py:169
  74.8 5.5 %collective-permute-start.5 = (bf16[128,2,128]{2,0,1:T(8,128)(2,1)S(1)}, bf16[128,2,128]{2,0,1:T(8,128)(2,1)S(1)}, u32[]{:S(2)}, u32[]{:S(2)}) collective-permute-start(bf16[128,2,128]{2,0,1:T(8,128)(2,1)S(1)} %get-tuple-element.319), channel_id=1, source_target_pairs={{0,12},{4,0},{8,4},{12,8},{1,13},{5,1},{9,5},{13,9},{2,14},{6,2},{... | collective-permute-start | bytes 196616 | tf_op jit(solution)/shard_map/ppermute | solution.py:141
  80.3 7.9 %collective-permute-start.6 = (bf16[128,2,256]{2,0,1:T(8,128)(2,1)S(1)}, bf16[128,2,256]{2,0,1:T(8,128)(2,1)S(1)}, u32[]{:S(2)}, u32[]{:S(2)}) collective-permute-start(bf16[128,2,256]{2,0,1:T(8,128)(2,1)S(1)} %pad_maximum_fusion.3), channel_id=1, source_target_pairs={{0,8},{4,12},{8,0},{12,4},{1,9},{5,13},{9,1},{13,5},{2,10},{6,14},... | collective-permute-start | bytes 393224 | tf_op jit(solution)/shard_map/ppermute | solution.py:141
Sparse Core Ops, SparseCore 0:
  56.1 10.9 reduce-scatter.2
  93.9 23.7 reduce-scatter.4
